TPU v7x, 32 devices: a whole 2x2x4 slice. The times are simulated.
32 devices in a mesh: groups: 2 (over x), space: 16 (over z, y, core).
Axes of the slice: x: 2, y: 2, z: 4, core: 2. Of those that a mesh axis runs over, the one named last changes fastest.
Arguments:
- prior_states: bfloat16 [2, 128, 8, 65536], P(None, None, None, ('groups', 'space')), parts along dimension 3, may hold values from -6 to 6
- mixing_matrix: bfloat16 [128, 256], P(None, 'groups'), parts along dimension 1, may hold values from -0.5 to 0.5
- capacity_factor: bfloat16 [8, 65536], P(None, ('groups', 'space')), parts along dimension 1, may hold values from 0.5 to 4
- live_flags: int32 [8, 65536], P(None, ('groups', 'space')), parts along dimension 1, may hold values 0 or 1
- borehole_block_location: int32 [8, 64], P(None, 'groups'), parts along dimension 1, may hold values from 0 to 32767
- borehole_injection_speed: float32 [8, 64], P(None, 'groups'), parts along dimension 1, may hold values from -8 to 8
Outputs:
- pressure: float32 [2048, 16, 8, 256], P(('groups', 'space')), parts along dimension 0
There are 2 independent parts, one for each index of `groups`. A program takes and returns all parts, laid end to end along the dimension named above; each array names one. Nothing has to cross between parts.
All inputs are finite; a program needn't handle non-finite values. No bound on the sum of `live_flags` on one device may be relied on, other than what follows from the above.
Results may differ from a plain program's by a relative error of at most 0.004.
Values may be sent and summed in bfloat16 or wider, within the bound.
A program may use at most 256 MiB of HBM per device.

v0:
```python
import jax
import jax.numpy as jnp
from jax import lax
from jax.sharding import PartitionSpec as P

SLAB_BLOCKS = 8
TX = 16
NZ = 8
NY = 256
SWEEPS = 3


def from_behind(block, axis, distance):
    devices = range(lax.axis_size(axis))
    route = [(i - distance, i) for i in devices if i - distance in devices]
    return lax.ppermute(block, axis, route)


def as_sent(shard):
    return jax.tree.map(lambda a: a.astype(jnp.bfloat16) if a.dtype == jnp.float32 else a, shard)


def mobility(value):
    return 1.0 / (1.0 + 0.25 * value * value)


def neighbours(padded):
    return (
        padded[..., 2:, 1:-1, 1:-1],
        padded[..., :-2, 1:-1, 1:-1],
        padded[..., 1:-1, 2:, 1:-1],
        padded[..., 1:-1, :-2, 1:-1],
        padded[..., 1:-1, 1:-1, 2:],
        padded[..., 1:-1, 1:-1, :-2],
    )


def combine(press_pad, flow_pad, storage_tile, start_field, source):
    flow_mid = flow_pad[..., 1:-1, 1:-1, 1:-1]
    numerator = storage_tile * start_field + source
    denominator = storage_tile
    for nb_press, nb_flow in zip(neighbours(press_pad), neighbours(flow_pad)):
        face_term = 0.5 * (flow_mid + nb_flow)
        numerator = numerator + face_term * nb_press
        denominator = denominator + face_term
    return numerator / denominator


def relax_sweep(
    pressure,
    perm_field,
    storage_tile,
    start_field,
    source,
    low_plane,
    high_plane,
    low_perm,
    high_perm,
):
    spread = ((0, 0), (0, 0), (1, 1), (1, 1))
    press_pad = jnp.pad(jnp.concatenate([low_plane, pressure, high_plane], axis=1), spread)
    flow_mid = perm_field * mobility(pressure)
    flow_pad = jnp.pad(
        jnp.concatenate(
            [low_perm * mobility(low_plane), flow_mid, high_perm * mobility(high_plane)], axis=1
        ),
        spread,
    )
    return combine(press_pad, flow_pad, storage_tile, start_field, source)


def on_device(
    prior_states,
    mixing_matrix,
    capacity_factor,
    live_flags,
    borehole_block_location,
    borehole_injection_speed,
):
    groups = lax.axis_size("space") // SLAB_BLOCKS
    members = mixing_matrix.shape[0]
    per_device = members // groups
    block_volume_list = prior_states.shape[3]
    tile_cells = TX * NZ * NY
    grid_shape = (per_device, TX, NZ, NY)
    realization_mixer = mixing_matrix.reshape(members, groups, per_device)
    analysis = jnp.einsum(
        "fpyc,pvm->yvfmc", prior_states, realization_mixer, preferred_element_type=jnp.float32
    ).astype(jnp.bfloat16)
    payload = analysis
    both_props = jnp.stack([capacity_factor, live_flags.astype(jnp.bfloat16)], axis=1)
    statics = jnp.broadcast_to(
        both_props[:, None, :, None, :], (SLAB_BLOCKS, groups, 2, 1, block_volume_list)
    )
    payload = payload.reshape(SLAB_BLOCKS * groups, 2, per_device, block_volume_list)
    statics = statics.reshape(SLAB_BLOCKS * groups, statics.shape[2], 1, block_volume_list)
    arrived, local_props = (
        lax.all_to_all(payload, "space", split_axis=0, concat_axis=3, tiled=True),
        lax.all_to_all(statics, "space", split_axis=0, concat_axis=3, tiled=True),
    )
    storage_tile = local_props[0, 0, 0].astype(jnp.float32).reshape(TX, NZ, NY)
    perm_bf = (
        local_props[0, 1, 0].astype(jnp.float32) * jnp.exp(arrived[0, 0].astype(jnp.float32))
    ).astype(jnp.bfloat16)
    perm_bf = perm_bf.reshape(grid_shape)
    perm_field = perm_bf.astype(jnp.float32)
    start_field = arrived[0, 1].astype(jnp.float32).reshape(grid_shape)
    tile_index = lax.axis_index("space") // groups
    well_index = lax.dynamic_index_in_dim(borehole_block_location, tile_index, 0, keepdims=False)
    well_flux = lax.dynamic_index_in_dim(borehole_injection_speed, tile_index, 0, keepdims=False)
    source = jnp.zeros((tile_cells,), jnp.float32).at[well_index].add(well_flux).reshape(TX, NZ, NY)
    pressure = start_field
    for sweep_index in range(SWEEPS):
        low_edge = from_behind(jnp.stack([pressure[:, -1:], perm_field[:, -1:]]), "space", groups)
        high_edge = from_behind(
            as_sent(jnp.stack([pressure[:, :1], perm_field[:, :1]])), "space", -groups
        )
        pressure = relax_sweep(
            pressure,
            perm_field,
            storage_tile,
            start_field,
            source,
            low_edge[0],
            high_edge[0],
            low_edge[1],
            high_edge[1],
        )
    return pressure


def solution(mesh):
    placed = (
        P(None, None, None, ("groups", "space")),
        P(None, "groups"),
        P(None, ("groups", "space")),
        P(None, ("groups", "space")),
        P(None, "groups"),
        P(None, "groups"),
    )
    return jax.shard_map(
        on_device,
        mesh=mesh,
        in_specs=placed,
        out_specs=P(("groups", "space"), None, None, None),
        check_vma=False,
    )
```

profile of v0, /device:TPU:17, one launch (start us, length us, event | category | flops | bytes accessed | tf_op | source)
XLA Modules:
  0.0 689.0 jit_solution(16073276418512011460)
XLA Ops:
  2.4 6.5 all-to-all-start
  9.8 17.5 %convert_bitcast_fusion = bf16[8,2,2,64,2048]{4,3,0,2,1:T(8,128)(2,1)} fusion(bf16[128,2,64,1,1]{0,2,4,3,1:T(8,128)(2,1)S(1)} %bitcast.132, bf16[2,128,8,2048]{3,2,1,0:T(8,128)(2,1)} %param.6), kind=kOutput, calls=%fused_computation.126 | convolution fusion | flops 1077936128 | bytes 16809984 | tf_op jit(solution)/shard_map/fpyc,pvm->yvfmc/dot_general | solution.py:87
  27.3 8.3 %copy.52 = bf16[8,2,2,64,2048]{4,3,2,1,0:T(8,128)(2,1)} copy(bf16[8,2,2,64,2048]{4,3,0,2,1:T(8,128)(2,1)} %convert_bitcast_fusion) | data formatting | bytes 16777216 | tf_op jit(solution)/shard_map/convert_element_type | solution.py:89
  35.6 6.7 all-to-all-start.1
  43.0 181.2 %all-to-all-done.1 = bf16[16,2,64,2048]{3,2,1,0:T(8,128)(2,1)} async-done(((bf16[16,2,64,2048]{3,2,1,0:T(8,128)(2,1)}), bf16[16,2,64,2048]{3,2,1,0:T(8,128)(2,1)}, u32[]{:S(2)}, u32[]{:S(2)}) %all-to-all-start.1) | async-done | bytes 8388640 | tf_op jit(solution)/shard_map/all_to_all | solution.py:98
  224.2 8.4 %copy.58 = bf16[1,16,2,8,8,2048]{5,4,1,3,2,0:T(8,128)(2,1)} copy(bf16[1,16,2,8,8,2048]{5,4,3,2,1,0:T(8,128)(2,1)} %bitcast.42) | data formatting | bytes 16777216 | tf_op jit(solution)/shard_map/all_to_all | solution.py:98
  237.3 4.5 convert_exponential_fusion
  243.8 9.2 %copy.60 = f32[8,8,128,256]{3,2,1,0:T(8,128)S(1)} copy(f32[8,8,128,256]{3,1,2,0:T(8,128)} %bitcast.129) | data formatting | bytes 16777216
  253.0 4.5 fusion.5
  267.9 31.3 %collective-permute-done = bf16[2,64,1,8,256]{4,3,1,2,0:T(8,128)(2,1)S(1)} collective-permute-done((bf16[2,64,1,8,256]{4,3,1,2,0:T(8,128)(2,1)S(1)}, bf16[2,64,1,8,256]{4,3,1,2,0:T(8,128)(2,1)S(1)}, u32[]{:S(2)}, u32[]{:S(2)}) %collective-permute-start) | collective-permute-done | bytes 524320 | tf_op jit(solution)/shard_map/ppermute | solution.py:16
  300.5 15.5 %select_maximum_fusion.8 = f32[64,18,10,258]{3,2,0,1:T(8,128)} fusion(f32[64,1,8,256]{3,2,0,1:T(8,128)S(1)} %fusion.87, f32[64,16,8,256]{3,2,0,1:T(8,128)} %copy-done.3, f32[64,1,8,256]{3,2,0,1:T(8,128)S(1)} %slice_bitcast_fusion.6), kind=kLoop, calls=%fused_computation.13 | loop fusion | flops 44582400 | bytes 21325824 | tf_op jit(solution)/shard_map/concatenate | solution.py:61
  317.4 13.9 %select_maximum_fusion.10 = f32[64,18,10,258]{3,2,0,1:T(8,128)} fusion(f32[64,1,8,256]{3,2,0,1:T(8,128)S(1)} %fusion.78, f32[64,16,8,256]{3,2,0,1:T(8,128)S(1)} %bitcast.120, f32[64,1,8,256]{3,2,0,1:T(8,128)S(1)} %fusion.71), kind=kLoop, calls=%fused_computation.15 | loop fusion | flops 44582400 | bytes 21325824 | tf_op jit(solution)/shard_map/concatenate | solution.py:64
  331.3 71.1 %fusion.8 = (f32[64,16,8,256]{3,2,0,1:T(8,128)}, f32[64,16,8,256]{3,2,0,1:T(8,128)}) fusion(bf16[64,16,8,256]{3,2,0,1:T(8,128)(2,1)} %copy-done.4, f32[64,18,10,258]{3,2,0,1:T(8,128)} %select_maximum_fusion.8, f32[64,16,8,256]{3,2,0,1:T(8,128)} %get-tuple-element.11, f32[64,18,10,258]{3,2,0,1:T(8,128)} %select_maximum_fusion.10, ...), kind=kLoop, calls=%fused_computation.28 | loop fusion | flops 90177536 | bytes 107216896 | tf_op jit(solution)/shard_map/mul | solution.py:62
  406.6 4.5 collective-permute-start.2
  411.1 32.6 %collective-permute-done.2 = bf16[2,64,1,8,256]{4,3,1,2,0:T(8,128)(2,1)S(1)} collective-permute-done((bf16[2,64,1,8,256]{4,3,1,2,0:T(8,128)(2,1)S(1)}, bf16[2,64,1,8,256]{4,3,1,2,0:T(8,128)(2,1)S(1)}, u32[]{:S(2)}, u32[]{:S(2)}) %collective-permute-start.2) | collective-permute-done | bytes 524320 | tf_op jit(solution)/shard_map/ppermute | solution.py:16
  443.9 15.8 %select_maximum_fusion.4 = f32[64,18,10,258]{3,2,0,1:T(8,128)} fusion(f32[64,1,8,256]{3,2,0,1:T(8,128)S(1)} %fusion.88, f32[64,16,8,256]{3,2,0,1:T(8,128)} %get-tuple-element.10, f32[64,1,8,256]{3,2,0,1:T(8,128)S(1)} %slice_bitcast_fusion.3), kind=kLoop, calls=%fused_computation.9 | loop fusion | flops 44582400 | bytes 21325824 | tf_op jit(solution)/shard_map/concatenate | solution.py:61
  459.9 13.9 %select_maximum_fusion.6 = f32[64,18,10,258]{3,2,0,1:T(8,128)} fusion(f32[64,1,8,256]{3,2,0,1:T(8,128)S(1)} %fusion.79, f32[64,16,8,256]{3,2,0,1:T(8,128)S(1)} %bitcast.124, f32[64,1,8,256]{3,2,0,1:T(8,128)S(1)} %fusion.74), kind=kLoop, calls=%fused_computation.11 | loop fusion | flops 44582400 | bytes 21325824 | tf_op jit(solution)/shard_map/concatenate | solution.py:64
  473.8 69.9 %fusion.11 = (f32[64,16,8,256]{3,2,0,1:T(8,128)}, f32[64,16,8,256]{3,2,0,1:T(8,128)}) fusion(bf16[64,16,8,256]{3,2,0,1:T(8,128)(2,1)} %copy-done.4, f32[64,18,10,258]{3,2,0,1:T(8,128)} %select_maximum_fusion.4, f32[64,16,8,256]{3,2,0,1:T(8,128)} %get-tuple-element.9, f32[64,18,10,258]{3,2,0,1:T(8,128)} %select_maximum_fusion.6, ...), kind=kLoop, calls=%fused_computation.31 | loop fusion | flops 92274688 | bytes 111411200 | tf_op jit(solution)/shard_map/mul | solution.py:62
  547.9 4.5 collective-permute-start.4
  552.4 32.6 %collective-permute-done.4 = bf16[2,64,1,8,256]{4,3,1,2,0:T(8,128)(2,1)S(1)} collective-permute-done((bf16[2,64,1,8,256]{4,3,1,2,0:T(8,128)(2,1)S(1)}, bf16[2,64,1,8,256]{4,3,1,2,0:T(8,128)(2,1)S(1)}, u32[]{:S(2)}, u32[]{:S(2)}) %collective-permute-start.4) | collective-permute-done | bytes 524320 | tf_op jit(solution)/shard_map/ppermute | solution.py:16
  585.2 15.8 %select_maximum_fusion = f32[64,18,10,258]{3,2,0,1:T(8,128)} fusion(f32[64,1,8,256]{3,2,0,1:T(8,128)S(1)} %fusion.89, f32[64,16,8,256]{3,2,0,1:T(8,128)} %get-tuple-element.8, f32[64,1,8,256]{3,2,0,1:T(8,128)S(1)} %slice_bitcast_fusion), kind=kLoop, calls=%fused_computation.5 | loop fusion | flops 44582400 | bytes 21325824 | tf_op jit(solution)/shard_map/concatenate | solution.py:61
  601.2 13.9 %select_maximum_fusion.2 = f32[64,18,10,258]{3,2,0,1:T(8,128)} fusion(f32[64,1,8,256]{3,2,0,1:T(8,128)S(1)} %fusion.80, f32[64,16,8,256]{3,2,0,1:T(8,128)S(1)} %bitcast.122, f32[64,1,8,256]{3,2,0,1:T(8,128)S(1)} %fusion.77), kind=kLoop, calls=%fused_computation.7 | loop fusion | flops 44582400 | bytes 21325824 | tf_op jit(solution)/shard_map/concatenate | solution.py:64
  615.1 65.7 %fusion.13 = f32[64,16,8,256]{3,2,0,1:T(8,128)} fusion(f32[64,18,10,258]{3,2,0,1:T(8,128)} %select_maximum_fusion, f32[64,16,8,256]{3,2,0,1:T(8,128)} %get-tuple-element.8, f32[64,1,8,256]{3,2,0,1:T(8,128)S(1)} %slice_bitcast_fusion, f32[64,1,8,256]{3,2,0,1:T(8,128)S(1)} %fusion.89, f32[64,16,8,256]{3,2,0,1:T(8,128)} %get-tuple-element.7, ...), kind=kLoop, calls=%fused_computation.34 | loop fusion | flops 79691776 | bytes 98828288 | tf_op jit(solution)/shard_map/div | solution.py:46
  680.7 8.0 %copy.56 = f32[64,16,8,256]{3,2,1,0:T(8,128)} copy(f32[64,16,8,256]{3,2,0,1:T(8,128)} %fusion.13) | data formatting | bytes 16777216 | tf_op jit(solution)/shard_map/div | solution.py:46
  (76 shorter events, 32.5 us)
Async XLA Ops:
  0.0 266.8 %copy-start = (f32[8,32]{1,0:T(8,128)S(1)}, f32[8,32]{1,0:T(8,128)}, u32[]{:S(2)}) copy-start(f32[8,32]{1,0:T(8,128)} %param.11) | copy-start | bytes 3076
  2.4 33.2 %all-to-all-start = ((bf16[16,2,1,2048]{3,1,2,0:T(2,128)(2,1)}), bf16[16,2,1,2048]{3,1,2,0:T(2,128)(2,1)S(1)}, u32[]{:S(2)}, u32[]{:S(2)}) async-start(bf16[16,2,1,2048]{3,1,2,0:T(2,128)(2,1)} %bitcast.2), calls=%async_computation | async-start | bytes 262144 | tf_op jit(solution)/shard_map/all_to_all | solution.py:99
  35.6 188.6 %all-to-all-start.1 = ((bf16[16,2,64,2048]{3,2,1,0:T(8,128)(2,1)}), bf16[16,2,64,2048]{3,2,1,0:T(8,128)(2,1)}, u32[]{:S(2)}, u32[]{:S(2)}) async-start(bf16[16,2,64,2048]{3,2,1,0:T(8,128)(2,1)} %bitcast.128), calls=%async_computation.1 | async-start | bytes 16777216 | tf_op jit(solution)/shard_map/all_to_all | solution.py:98
  232.6 4.6 copy-start.5
  242.9 10.1 %copy-start.2 = (bf16[8,8,128,256]{3,2,1,0:T(8,128)(2,1)}, bf16[8,8,128,256]{3,2,1,0:T(8,128)(2,1)S(1)}, u32[]{:S(2)}) copy-start(bf16[8,8,128,256]{3,2,1,0:T(8,128)(2,1)S(1)} %copy.59) | copy-start | bytes 12582916
  243.8 14.6 %copy-start.3 = (f32[64,16,8,256]{3,2,0,1:T(8,128)}, f32[64,16,8,256]{3,2,0,1:T(8,128)S(1)}, u32[]{:S(2)}) copy-start(f32[64,16,8,256]{3,2,0,1:T(8,128)S(1)} %copy_convert_fusion) | copy-start | bytes 25165828
  257.5 2.4 copy-start.4
  259.8 39.4 %collective-permute-start.1 = (f32[2,64,1,8,256]{4,3,1,2,0:T(8,128)}, f32[2,64,1,8,256]{4,3,1,2,0:T(8,128)}, u32[]{:S(2)}, u32[]{:S(2)}) collective-permute-start(f32[2,64,1,8,256]{4,3,1,2,0:T(8,128)} %pad_maximum_fusion.14), channel_id=1, source_target_pairs={{0,2},{1,3},{2,4},{3,5},{4,6},{5,7},{6,8},{7,9},{8,10},{9,11},{10,... | collective-permute-start | bytes 3145736 | tf_op jit(solution)/shard_map/ppermute | solution.py:16
  261.8 37.3 %collective-permute-start = (bf16[2,64,1,8,256]{4,3,1,2,0:T(8,128)(2,1)S(1)}, bf16[2,64,1,8,256]{4,3,1,2,0:T(8,128)(2,1)S(1)}, u32[]{:S(2)}, u32[]{:S(2)}) collective-permute-start(bf16[2,64,1,8,256]{4,3,1,2,0:T(8,128)(2,1)S(1)} %pad_maximum_fusion.17), channel_id=1, source_target_pairs={{2,0},{3,1},{4,2},{5,3},{6,4},{7,5},{8,6},{9,7},{10,8},{11,9},{12,... | collective-permute-start | bytes 1572872 | tf_op jit(solution)/shard_map/ppermute | solution.py:16
  299.3 18.1 %slice-start = ((s8[8388608]{0:T(1024)(128)(4,1)}), s8[4194304]{0:T(1024)(128)(4,1)S(1)}, s32[]{:S(2)}) async-start(s8[8388608]{0:T(1024)(128)(4,1)} %bitcast.119), calls=%async_computation.2 | async-start | bytes 8388608
  300.5 16.8 %slice-start.1 = ((s8[8388608]{0:T(1024)(128)(4,1)}), s8[4194304]{0:T(1024)(128)(4,1)S(1)}, s32[]{:S(2)}) async-start(s8[8388608]{0:T(1024)(128)(4,1)} %bitcast.119), calls=%async_computation.3 | async-start | bytes 8388608
  404.6 39.2 %collective-permute-start.3 = (f32[2,64,1,8,256]{4,3,1,2,0:T(8,128)S(1)}, f32[2,64,1,8,256]{4,3,1,2,0:T(8,128)S(1)}, u32[]{:S(2)}, u32[]{:S(2)}) collective-permute-start(f32[2,64,1,8,256]{4,3,1,2,0:T(8,128)S(1)} %pad_maximum_fusion.13), channel_id=1, source_target_pairs={{0,2},{1,3},{2,4},{3,5},{4,6},{5,7},{6,8},{7,9},{8,10},{9,11},{10,... | collective-permute-start | bytes 3145736 | tf_op jit(solution)/shard_map/ppermute | solution.py:16
  406.6 37.1 %collective-permute-start.2 = (bf16[2,64,1,8,256]{4,3,1,2,0:T(8,128)(2,1)S(1)}, bf16[2,64,1,8,256]{4,3,1,2,0:T(8,128)(2,1)S(1)}, u32[]{:S(2)}, u32[]{:S(2)}) collective-permute-start(bf16[2,64,1,8,256]{4,3,1,2,0:T(8,128)(2,1)S(1)} %pad_maximum_fusion.16), channel_id=1, source_target_pairs={{2,0},{3,1},{4,2},{5,3},{6,4},{7,5},{8,6},{9,7},{10,8},{11,9},{12,... | collective-permute-start | bytes 1572872 | tf_op jit(solution)/shard_map/ppermute | solution.py:16
  443.9 16.0 %slice-start.4 = ((s8[8388608]{0:T(1024)(128)(4,1)}), s8[4194304]{0:T(1024)(128)(4,1)S(1)}, s32[]{:S(2)}) async-start(s8[8388608]{0:T(1024)(128)(4,1)} %bitcast.123), calls=%async_computation.6 | async-start | bytes 8388608
  443.9 15.9 %slice-start.5 = ((s8[8388608]{0:T(1024)(128)(4,1)}), s8[4194304]{0:T(1024)(128)(4,1)S(1)}, s32[]{:S(2)}) async-start(s8[8388608]{0:T(1024)(128)(4,1)} %bitcast.123), calls=%async_computation.7 | async-start | bytes 8388608
  545.9 39.2 %collective-permute-start.5 = (f32[2,64,1,8,256]{4,3,1,2,0:T(8,128)S(1)}, f32[2,64,1,8,256]{4,3,1,2,0:T(8,128)S(1)}, u32[]{:S(2)}, u32[]{:S(2)}) collective-permute-start(f32[2,64,1,8,256]{4,3,1,2,0:T(8,128)S(1)} %pad_maximum_fusion.12), channel_id=1, source_target_pairs={{0,2},{1,3},{2,4},{3,5},{4,6},{5,7},{6,8},{7,9},{8,10},{9,11},{10,... | collective-permute-start | bytes 3145736 | tf_op jit(solution)/shard_map/ppermute | solution.py:16
  547.9 37.1 %collective-permute-start.4 = (bf16[2,64,1,8,256]{4,3,1,2,0:T(8,128)(2,1)S(1)}, bf16[2,64,1,8,256]{4,3,1,2,0:T(8,128)(2,1)S(1)}, u32[]{:S(2)}, u32[]{:S(2)}) collective-permute-start(bf16[2,64,1,8,256]{4,3,1,2,0:T(8,128)(2,1)S(1)} %pad_maximum_fusion.15), channel_id=1, source_target_pairs={{2,0},{3,1},{4,2},{5,3},{6,4},{7,5},{8,6},{9,7},{10,8},{11,9},{12,... | collective-permute-start | bytes 1572872 | tf_op jit(solution)/shard_map/ppermute | solution.py:16
  585.2 16.0 %slice-start.2 = ((s8[8388608]{0:T(1024)(128)(4,1)}), s8[4194304]{0:T(1024)(128)(4,1)S(1)}, s32[]{:S(2)}) async-start(s8[8388608]{0:T(1024)(128)(4,1)} %bitcast.121), calls=%async_computation.4 | async-start | bytes 8388608
  585.2 15.9 %slice-start.3 = ((s8[8388608]{0:T(1024)(128)(4,1)}), s8[4194304]{0:T(1024)(128)(4,1)S(1)}, s32[]{:S(2)}) async-start(s8[8388608]{0:T(1024)(128)(4,1)} %bitcast.121), calls=%async_computation.5 | async-start | bytes 8388608
  615.1 73.7 %copy-start.1 = (f32[8,32]{1,0:T(8,128)S(1)}, f32[8,32]{1,0:T(8,128)}, u32[]{:S(2)}) copy-start(f32[8,32]{1,0:T(8,128)} %param.11) | copy-start | bytes 3076
where the time goes:
time: 698 us; the launch traced here: 689 us
  other arithmetic  314 us (45%)
  waiting for transfers between devices  278 us (40%)
  local copies, waits for them, and re-layouts  47.3 us (7%)
  starting transfers between devices  32.2 us (5%)
  matrix products  17.5 us (3%)
    all_to_all x1, waiting for transfers between devices, on_device(): lax.all_to_all(payload, 'space', split_axis=0, concat_axis=3, tiled=True)  181 us
    mul x3, other arithmetic, relax_sweep(): flow_mid = perm_field * mobility(pressure)  145 us
    ppermute x6, waiting for transfers between devices, from_behind(): return lax.ppermute(block, axis, route)  96.5 us
    div x1, other arithmetic, combine(): return numerator / denominator  65.7 us
    concatenate x3, other arithmetic, relax_sweep(): jnp.concatenate([low_plane, pressure, high_plane], axis=1)  47.2 us
    concatenate x3, other arithmetic, relax_sweep(): jnp.concatenate([low_perm * mobility(low_plane), flow_mid, high_perm * mo...  41.7 us
    ppermute x6, starting transfers between devices, from_behind(): return lax.ppermute(block, axis, route)  19 us
    dot_general x1, matrix products, on_device(): jnp.einsum('fpyc,pvm->yvfmc', prior_states, realization_mixer, preferred_...  17.5 us
  transfers between devices with their start and end apart: 8, of which 4 were waited for; matrix products, arithmetic and copies ran while one was open for 4% of the time, Pallas kernels for 0%

commit v1 on v0

v1 whole, which is shorter than its diff:
```python
import functools

import jax
import jax.numpy as jnp
from jax import lax
from jax.experimental import pallas as pl
from jax.experimental.pallas import tpu as pltpu
from jax.sharding import PartitionSpec as P

SLAB_BLOCKS = 8
TX = 16
NZ = 8
NY = 256
SWEEPS = 3
PLANE = NZ * NY
HALO = SWEEPS
PADDED = TX + 2 * HALO
CHUNK = 8
MESH = pl.DeviceIdType.MESH


def kernel(
    space,
    members,
    piece,
    depth,
    prior_ref,
    mix_ref,
    cap_ref,
    live_ref,
    where_ref,
    speed_ref,
    out_ref,
    weights,
    states,
    send,
    recv,
    result,
    press,
    flow,
    carried,
    storage,
    source,
    source_rows,
    cap_send,
    cap_recv,
    state_sem,
    send_sem,
    recv_sem,
    halo_send_sem,
    halo_recv_sem,
    cap_send_sem,
    cap_recv_sem,
    edge_send_sem,
    edge_recv_sem,
    out_sem,
):
    groups = space // SLAB_BLOCKS
    share = members // groups
    chunks = share // CHUNK
    rows_z = piece // NY
    per_plane = PLANE // piece
    pieces = TX * per_plane
    edge = HALO * per_plane

    me = lax.axis_index("space")
    tile = me // groups
    wells = where_ref.shape[1]

    barrier = pltpu.get_barrier_semaphore()

    @pl.loop(1, space)
    def _(d):
        pl.semaphore_signal(
            barrier, inc=1, device_id={"space": lax.rem(me + d, space)}, device_id_type=MESH
        )

    def state_copy(i):
        t = lax.rem(tile + SLAB_BLOCKS // 2 + i, SLAB_BLOCKS)
        slot = lax.rem(i, 2)
        return pltpu.make_async_copy(prior_ref.at[t], states.at[slot], state_sem.at[slot])

    state_copy(0).start()
    weights[...] = mix_ref[...].astype(jnp.float32).T.astype(jnp.bfloat16)
    caps = cap_ref[...].astype(jnp.float32)
    for t in range(SLAB_BLOCKS):
        cap_send[t] = caps[t : t + 1, :]

    @pl.when(tile == 0)
    def _():
        @pl.loop(0, chunks)
        def _(c):
            for j in range(edge):
                recv[c, j] = jnp.zeros_like(recv[c, j])

        for b in range(2):
            for j in range(HALO):
                for ref in (press, flow, carried):
                    ref[b, j] = jnp.zeros_like(ref[b, j])

    @pl.when(tile == SLAB_BLOCKS - 1)
    def _():
        @pl.loop(0, chunks)
        def _(c):
            for j in range(edge):
                recv[c, edge + pieces + j] = jnp.zeros_like(recv[c, j])

        for b in range(2):
            for j in range(HALO):
                for ref in (press, flow, carried):
                    ref[b, HALO + TX + j] = jnp.zeros_like(ref[b, j])

    pl.semaphore_wait(barrier, space - 1)

    def send_piece(c, dest):
        @pl.when(dest != me)
        def _():
            pltpu.make_async_remote_copy(
                src_ref=send.at[c, dest],
                dst_ref=recv.at[c, edge + me],
                send_sem=send_sem.at[c],
                recv_sem=recv_sem.at[c],
                device_id={"space": dest},
                device_id_type=MESH,
            ).start()

        @pl.when(dest == me)
        def _():
            pltpu.make_async_copy(
                send.at[c, dest], recv.at[c, edge + me], recv_sem.at[c]
            ).start()

    def send_chunk(c):
        @pl.loop(0, space)
        def _(d):
            send_piece(c, lax.rem(me + space // 2 + d, space))

    @pl.loop(0, space)
    def _(d):
        dest = lax.rem(me + d, space)

        @pl.when(dest != me)
        def _():
            pltpu.make_async_remote_copy(
                src_ref=cap_send.at[dest // groups],
                dst_ref=cap_recv.at[edge + me],
                send_sem=cap_send_sem,
                recv_sem=cap_recv_sem,
                device_id={"space": dest},
                device_id_type=MESH,
            ).start()

        @pl.when(dest == me)
        def _():
            pltpu.make_async_copy(
                cap_send.at[dest // groups], cap_recv.at[edge + me], cap_recv_sem
            ).start()

    def edges(buffer, send_sems, recv_sems):
        up = pltpu.make_async_remote_copy(
            src_ref=buffer.at[pl.ds(pieces, edge)],
            dst_ref=buffer.at[pl.ds(0, edge)],
            send_sem=send_sems.at[0],
            recv_sem=recv_sems.at[0],
            device_id={"space": lax.rem(me + groups, space)},
            device_id_type=MESH,
        )
        down = pltpu.make_async_remote_copy(
            src_ref=buffer.at[pl.ds(edge, edge)],
            dst_ref=buffer.at[pl.ds(edge + pieces, edge)],
            send_sem=send_sems.at[1],
            recv_sem=recv_sems.at[1],
            device_id={"space": lax.rem(me + space - groups, space)},
            device_id_type=MESH,
        )
        return up, down

    def start_edges(*args):
        up, down = edges(*args)

        @pl.when(tile < SLAB_BLOCKS - 1)
        def _():
            up.start()

        @pl.when(tile > 0)
        def _():
            down.start()

    def wait_edges(*args):
        up, down = edges(*args)

        @pl.when(tile > 0)
        def _():
            up.wait_recv()

        @pl.when(tile < SLAB_BLOCKS - 1)
        def _():
            down.wait_recv()

    def wait_edges_sent(*args):
        up, down = edges(*args)

        @pl.when(tile < SLAB_BLOCKS - 1)
        def _():
            up.wait_send()

        @pl.when(tile > 0)
        def _():
            down.wait_send()

    cap_edges = (cap_recv, edge_send_sem, edge_recv_sem)

    @pl.loop(0, SLAB_BLOCKS)
    def _(i):
        t = lax.rem(tile + SLAB_BLOCKS // 2 + i, SLAB_BLOCKS)
        slot = lax.rem(i, 2)

        @pl.when(i + 1 < SLAB_BLOCKS)
        def _():
            state_copy(i + 1).start()

        state_copy(i).wait()
        for j in range(rows_z):
            lanes = pl.ds(j * NY, NY)
            logs = jnp.dot(
                weights[...], states[slot, 0, :, lanes], preferred_element_type=jnp.float32
            )
            start = jnp.dot(
                weights[...], states[slot, 1, :, lanes], preferred_element_type=jnp.float32
            )
            live = live_ref[pl.ds(t, 1), lanes].astype(jnp.float32)
            perm = live * jnp.exp(logs.astype(jnp.bfloat16).astype(jnp.float32))
            for v in range(groups):
                for c in range(chunks):
                    r = v * share + c * CHUNK
                    both = jnp.concatenate([perm[r : r + CHUNK], start[r : r + CHUNK]], axis=0)
                    send[c, t * groups + v, :, lanes] = both.astype(jnp.bfloat16)

        @pl.loop(0, groups)
        def _(v):
            send_piece(0, t * groups + v)

        @pl.when(i == 2)
        def _():
            pltpu.make_async_copy(
                cap_recv.at[pl.ds(edge, pieces)], cap_recv.at[pl.ds(edge, pieces)], cap_recv_sem
            ).wait()
            start_edges(*cap_edges)

    @pl.loop(1, min(depth, chunks))
    def _(c):
        send_chunk(c)

    source_rows[...] = jnp.zeros_like(source_rows)
    cell = lax.broadcasted_iota(jnp.int32, source_rows.shape, 0) * PLANE
    cell = cell + lax.broadcasted_iota(jnp.int32, source_rows.shape, 1)

    @pl.loop(0, wells)
    def _(w):
        for shift in (-1, 0, 1):
            t = jnp.clip(tile + shift, 0, SLAB_BLOCKS - 1)
            spot = where_ref[t, w] + (HALO + shift * TX) * PLANE
            rate = speed_ref[t, w] * (1.0 / 16.0)
            source_rows[...] += jnp.where(cell == spot, rate, 0.0)

    wait_edges(*cap_edges)

    for x in range(PADDED):
        for z in range(NZ):
            held = cap_recv[
                x * per_plane + z // rows_z, :, (z % rows_z) * NY : (z % rows_z + 1) * NY
            ]
            storage[x, z] = jnp.broadcast_to(held * (1.0 / 16.0), (CHUNK, NY))
            source[x, z] = jnp.broadcast_to(
                source_rows[x : x + 1, z * NY : (z + 1) * NY], (CHUNK, NY)
            )

    lane = lax.broadcasted_iota(jnp.int32, (CHUNK, NY), 1)
    first, last = lane == 0, lane == NY - 1

    def fields(c, x, z):
        both = recv[
            c, x * per_plane + z // rows_z, :, pl.ds((z % rows_z) * NY, NY)
        ].astype(jnp.float32)
        return both[:CHUNK], both[CHUNK:]

    def keep(b, x, z, p, perm):
        h = perm / (32.0 + 8.0 * p * p)
        press[b, x, z] = p
        flow[b, x, z] = h
        carried[b, x, z] = h * p

    def updated(b, x, z, start):
        p, h = press[b, x, z], flow[b, x, z]
        sides = [(x - 1, z), (x + 1, z)]
        if z > 0:
            sides.append((x, z - 1))
        if z < NZ - 1:
            sides.append((x, z + 1))
        p_left = jnp.where(first, 0.0, pltpu.roll(p, 1, 1))
        h_left = jnp.where(first, 0.0, pltpu.roll(h, 1, 1))
        p_right = jnp.where(last, 0.0, pltpu.roll(p, NY - 1, 1))
        h_right = jnp.where(last, 0.0, pltpu.roll(h, NY - 1, 1))
        p_sum = p_left + p_right
        h_sum = h_left + h_right
        hp_sum = h_left * p_left + h_right * p_right
        for at in sides:
            p_sum = p_sum + press[(b,) + at]
            h_sum = h_sum + flow[(b,) + at]
            hp_sum = hp_sum + carried[(b,) + at]
        s = storage[x, z]
        above = s * start + source[x, z] + h * p_sum + hp_sum
        below = s + 6.0 * h + h_sum
        return above / below

    def relax(c):
        @pl.loop(0, PADDED)
        def _(x):
            for z in range(NZ):
                perm, start = fields(c, x, z)
                keep(0, x, z, start, perm)

        for sweep in range(SWEEPS):
            b = sweep % 2
            reach = SWEEPS - 1 - sweep
            low = HALO - jnp.where(tile == 0, 0, reach)
            high = HALO + TX + jnp.where(tile == SLAB_BLOCKS - 1, 0, reach)

            def plane(x, _, b=b, sweep=sweep):
                for z in range(NZ):
                    perm, start = fields(c, x, z)
                    p = updated(b, x, z, start)
                    if sweep < SWEEPS - 1:
                        keep(1 - b, x, z, p, perm)
                    else:
                        result[c, x - HALO, z] = p
                return 0

            lax.fori_loop(low, high, plane, 0)

    def out_copy(c):
        return pltpu.make_async_copy(
            result.at[c], out_ref.at[:, :, pl.ds(c * CHUNK, CHUNK), :], out_sem.at[c]
        )

    def halo(c):
        return recv.at[c], halo_send_sem.at[c], halo_recv_sem.at[c]

    @pl.loop(0, chunks + 1)
    def _(c):
        @pl.when(c < chunks)
        def _():
            got = recv.at[c, pl.ds(edge, pieces)]
            pltpu.make_async_copy(got, got, recv_sem.at[c]).wait()
            start_edges(*halo(c))

        @pl.when(c + depth < chunks)
        def _():
            send_chunk(c + depth)

        @pl.when(c > 0)
        def _():
            wait_edges(*halo(c - 1))
            relax(c - 1)
            out_copy(c - 1).start()

    @pl.loop(0, chunks)
    def _(c):
        sent = send.at[c, pl.ds(0, space - 1)]
        pltpu.make_async_copy(sent, sent, send_sem.at[c]).wait()
        wait_edges_sent(*halo(c))
        out_copy(c).wait()

    sent = cap_recv.at[pl.ds(0, space - 1)]
    pltpu.make_async_copy(sent, sent, cap_send_sem).wait()
    wait_edges_sent(*cap_edges)


def on_device(
    prior_states,
    mixing_matrix,
    capacity_factor,
    live_flags,
    borehole_block_location,
    borehole_injection_speed,
):
    space = lax.axis_size("space")
    groups = space // SLAB_BLOCKS
    members = mixing_matrix.shape[0]
    share = members // groups
    chunks = share // CHUNK
    piece = prior_states.shape[3]
    per_plane = PLANE // piece
    padded_pieces = PADDED * per_plane
    by_tile = prior_states.transpose(2, 0, 1, 3)
    vmem = pl.BlockSpec(memory_space=pltpu.VMEM)
    smem = pl.BlockSpec(memory_space=pltpu.SMEM)
    hbm = pl.BlockSpec(memory_space=pl.ANY)
    dma = pltpu.SemaphoreType.DMA
    slab = (PADDED, NZ, CHUNK, NY)
    out = pl.pallas_call(
        functools.partial(kernel, space, members, piece, 2),
        out_shape=jax.ShapeDtypeStruct((TX, NZ, share, NY), jnp.float32),
        in_specs=[hbm, vmem, vmem, vmem, smem, smem],
        out_specs=hbm,
        scratch_shapes=[
            pltpu.VMEM((members, members), jnp.bfloat16),
            pltpu.VMEM((2, 2, members, piece), jnp.bfloat16),
            pltpu.VMEM((chunks, space, 2 * CHUNK, piece), jnp.bfloat16),
            pltpu.VMEM((chunks, padded_pieces, 2 * CHUNK, piece), jnp.bfloat16),
            pltpu.VMEM((chunks, TX, NZ, CHUNK, NY), jnp.float32),
            pltpu.VMEM((2,) + slab, jnp.float32),
            pltpu.VMEM((2,) + slab, jnp.float32),
            pltpu.VMEM((2,) + slab, jnp.float32),
            pltpu.VMEM(slab, jnp.float32),
            pltpu.VMEM(slab, jnp.float32),
            pltpu.VMEM((-(-PADDED // 8) * 8, PLANE), jnp.float32),
            pltpu.VMEM((SLAB_BLOCKS, 1, piece), jnp.float32),
            pltpu.VMEM((padded_pieces, 1, piece), jnp.float32),
            dma((2,)),
            dma((chunks,)),
            dma((chunks,)),
            dma((chunks, 2)),
            dma((chunks, 2)),
            dma(()),
            dma(()),
            dma((2,)),
            dma((2,)),
            dma((chunks,)),
        ],
        compiler_params=pltpu.CompilerParams(
            collective_id=0, has_side_effects=True, vmem_limit_bytes=56 * 1024 * 1024
        ),
    )(
        by_tile,
        mixing_matrix,
        capacity_factor,
        live_flags,
        borehole_block_location,
        borehole_injection_speed,
    )
    return out.transpose(2, 0, 1, 3)


def solution(mesh):
    placed = (
        P(None, None, None, ("groups", "space")),
        P(None, "groups"),
        P(None, ("groups", "space")),
        P(None, ("groups", "space")),
        P(None, "groups"),
        P(None, "groups"),
    )
    return jax.shard_map(
        on_device,
        mesh=mesh,
        in_specs=placed,
        out_specs=P(("groups", "space"), None, None, None),
        check_vma=False,
    )
```

time: 698 us -> 274 us (0.39)
  other arithmetic: 314 us -> 0 us
  waiting for transfers between devices: 278 us -> 0 us
  Pallas kernels: 0 us -> 248 us
  starting transfers between devices: 32.2 us -> 0 us
  local copies, waits for them, and re-layouts: 47.3 us -> 23 us
  matrix products: 17.5 us -> 0 us
    pallas_call x0 -> x1, Pallas kernels: none -> 248 us  [on_device(): pl.pallas_call(functools.partial(kernel, space, members, piece, 2), out_s...]
    all_to_all x2 -> x0, waiting for transfers between devices: 181 us -> none  [the longest x1 181 us: on_device(): lax.all_to_all(payload, 'space', split_axis=0, concat_axis=3, tiled=True)]
    mul x6 -> x0, other arithmetic: 147 us -> none  [the longest x3 145 us: relax_sweep(): flow_mid = perm_field * mobility(pressure)]
    ppermute x6 -> x0, waiting for transfers between devices: 96.5 us -> none  [from_behind(): return lax.ppermute(block, axis, route)]
    concatenate x6 -> x0, other arithmetic: 88.8 us -> none  [the longest x3 47.2 us: relax_sweep(): jnp.concatenate([low_plane, pressure, high_plane], axis=1)]
    div x1 -> x0, other arithmetic: 65.7 us -> none  [combine(): return numerator / denominator]
    ppermute x6 -> x0, starting transfers between devices: 19 us -> none  [from_behind(): return lax.ppermute(block, axis, route)]
    dot_general x1 -> x0, matrix products: 17.5 us -> none  [on_device(): jnp.einsum('fpyc,pvm->yvfmc', prior_states, realization_mixer, preferred_...]
  transfers between devices with their start and end apart: 8 -> 0, of which waited for: 4 -> 0; matrix products, arithmetic and copies ran while one was open for 4% -> 0% of each run, Pallas kernels for 0% -> 0%
where the time goes in v1:
time: 274 us; the launch traced here: 271 us
  Pallas kernels  248 us (91%)
  local copies, waits for them, and re-layouts  23 us (8%)
    pallas_call x1, Pallas kernels, on_device(): pl.pallas_call(functools.partial(kernel, space, members, piece, 2), out_s...  248 us
    transpose x1, local copies, waits for them, and re-layouts, on_device(): return out.transpose(2, 0, 1, 3)  11.6 us
    unnamed x1, local copies, waits for them, and re-layouts  11.4 us

profile of v1, /device:TPU:17, one launch (start us, length us, event | category | flops | bytes accessed | tf_op | source)
XLA Modules:
  0.0 271.4 jit_solution(11244065989095841951)
XLA Ops:
  0.0 11.4 %copy.10 = bf16[2,128,8,2048]{3,1,0,2:T(8,128)(2,1)} copy(bf16[2,128,8,2048]{3,2,1,0:T(8,128)(2,1)} %param.6) | data formatting | bytes 16777216 | tf_op args[0]
  11.4 248.3 %shard_map.64 = f32[16,8,64,256]{3,2,1,0:T(8,128)} custom-call(bf16[8,2,128,2048]{3,2,1,0:T(8,128)(2,1)} %bitcast.5, bf16[128,128]{1,0:T(8,128)(2,1)} %mix_ref.1, bf16[8,2048]{1,0:T(8,128)(2,1)} %cap_ref.1, s32[8,2048]{1,0:T(8,128)} %live_ref.1, s32[8,32]{1,0:T(8,128)} %where_ref.1, f32[8,32]{1,0:T(8,128)} %speed_ref.1), custom_call_target="tpu_custom_call" | custom-call | tf_op jit(solution)/shard_map/pallas_call | solution.py:401
  259.7 11.6 %copy.8 = f32[64,16,8,256]{3,2,1,0:T(8,128)} copy(f32[64,16,8,256]{3,0,2,1:T(8,128)} %bitcast.4) | data formatting | bytes 16777216 | tf_op jit(solution)/shard_map/transpose | solution.py:442

commit v2 on v1

--- a/solution.py
+++ b/solution.py
@@ -17,6 +17,13 @@
 PADDED = TX + 2 * HALO
 CHUNK = 8
 MESH = pl.DeviceIdType.MESH
+
+
+def turn(mine, i, count):
+    half = count // 2
+    here = mine // half
+    side = lax.rem(here + i + 1, 2)
+    return side * half + lax.rem(mine + i // 2, half)
 
 
 def kernel(
@@ -54,6 +61,7 @@
     edge_send_sem,
     edge_recv_sem,
     out_sem,
+    middle_sem,
 ):
     groups = space // SLAB_BLOCKS
     share = members // groups
@@ -76,7 +84,7 @@
         )
 
     def state_copy(i):
-        t = lax.rem(tile + SLAB_BLOCKS // 2 + i, SLAB_BLOCKS)
+        t = turn(tile, i, SLAB_BLOCKS)
         slot = lax.rem(i, 2)
         return pltpu.make_async_copy(prior_ref.at[t], states.at[slot], state_sem.at[slot])
 
@@ -130,10 +138,41 @@
                 send.at[c, dest], recv.at[c, edge + me], recv_sem.at[c]
             ).start()
 
+    middle = SLAB_BLOCKS // 2
+    owns_first = me < edge
+    owns_last = me >= pieces - edge
+
+    def send_middle(c):
+        for v in range(groups):
+
+            @pl.when(owns_first)
+            def _(v=v):
+                pltpu.make_async_remote_copy(
+                    src_ref=send.at[c, middle * groups + v],
+                    dst_ref=recv.at[c, edge + pieces + lax.rem(me, edge)],
+                    send_sem=middle_sem.at[c],
+                    recv_sem=halo_recv_sem.at[c, 1],
+                    device_id={"space": (middle - 1) * groups + v},
+                    device_id_type=MESH,
+                ).start()
+
+            @pl.when(owns_last)
+            def _(v=v):
+                pltpu.make_async_remote_copy(
+                    src_ref=send.at[c, (middle - 1) * groups + v],
+                    dst_ref=recv.at[c, lax.rem(me + edge - (pieces - edge) % edge, edge)],
+                    send_sem=middle_sem.at[c],
+                    recv_sem=halo_recv_sem.at[c, 0],
+                    device_id={"space": middle * groups + v},
+                    device_id_type=MESH,
+                ).start()
+
     def send_chunk(c):
         @pl.loop(0, space)
         def _(d):
-            send_piece(c, lax.rem(me + space // 2 + d, space))
+            send_piece(c, turn(me, d, space))
+
+        send_middle(c)
 
     @pl.loop(0, space)
     def _(d):
@@ -175,14 +214,19 @@
         )
         return up, down
 
-    def start_edges(*args):
+    sends_up = {False: tile < SLAB_BLOCKS - 1}
+    sends_up[True] = jnp.logical_and(sends_up[False], tile != middle - 1)
+    sends_down = {False: tile > 0}
+    sends_down[True] = jnp.logical_and(sends_down[False], tile != middle)
+
+    def start_edges(*args, direct=False):
         up, down = edges(*args)
 
-        @pl.when(tile < SLAB_BLOCKS - 1)
+        @pl.when(sends_up[direct])
         def _():
             up.start()
 
-        @pl.when(tile > 0)
+        @pl.when(sends_down[direct])
         def _():
             down.start()
 
@@ -197,14 +241,14 @@
         def _():
             down.wait_recv()
 
-    def wait_edges_sent(*args):
+    def wait_edges_sent(*args, direct=False):
         up, down = edges(*args)
 
-        @pl.when(tile < SLAB_BLOCKS - 1)
+        @pl.when(sends_up[direct])
         def _():
             up.wait_send()
 
-        @pl.when(tile > 0)
+        @pl.when(sends_down[direct])
         def _():
             down.wait_send()
 
@@ -212,7 +256,7 @@
 
     @pl.loop(0, SLAB_BLOCKS)
     def _(i):
-        t = lax.rem(tile + SLAB_BLOCKS // 2 + i, SLAB_BLOCKS)
+        t = turn(tile, i, SLAB_BLOCKS)
         slot = lax.rem(i, 2)
 
         @pl.when(i + 1 < SLAB_BLOCKS)
@@ -246,6 +290,8 @@
                 cap_recv.at[pl.ds(edge, pieces)], cap_recv.at[pl.ds(edge, pieces)], cap_recv_sem
             ).wait()
             start_edges(*cap_edges)
+
+    send_middle(0)
 
     @pl.loop(1, min(depth, chunks))
     def _(c):
@@ -352,7 +398,7 @@
         def _():
             got = recv.at[c, pl.ds(edge, pieces)]
             pltpu.make_async_copy(got, got, recv_sem.at[c]).wait()
-            start_edges(*halo(c))
+            start_edges(*halo(c), direct=True)
 
         @pl.when(c + depth < chunks)
         def _():
@@ -368,7 +414,13 @@
     def _(c):
         sent = send.at[c, pl.ds(0, space - 1)]
         pltpu.make_async_copy(sent, sent, send_sem.at[c]).wait()
-        wait_edges_sent(*halo(c))
+        wait_edges_sent(*halo(c), direct=True)
+        sent_too = send.at[c, pl.ds(0, groups)]
+
+        @pl.when(jnp.logical_or(owns_first, owns_last))
+        def _():
+            pltpu.make_async_copy(sent_too, sent_too, middle_sem.at[c]).wait()
+
         out_copy(c).wait()
 
     sent = cap_recv.at[pl.ds(0, space - 1)]
@@ -427,6 +479,7 @@
             dma((2,)),
             dma((2,)),
             dma((chunks,)),
+            dma((chunks,)),
         ],
         compiler_params=pltpu.CompilerParams(
             collective_id=0, has_side_effects=True, vmem_limit_bytes=56 * 1024 * 1024

time: 274 us -> 249 us (0.909)
  the two profiles are of different devices: /device:TPU:17 before, /device:TPU:5 now
where the time goes in v2:
time: 249 us
  Pallas kernels  226 us (91%)
  local copies, waits for them, and re-layouts  23 us (9%)
    pallas_call x1, Pallas kernels, on_device(): pl.pallas_call(functools.partial(kernel, space, members, piece, 2), out_s...  226 us
    transpose x1, local copies, waits for them, and re-layouts, on_device(): return out.transpose(2, 0, 1, 3)  11.6 us
    unnamed x1, local copies, waits for them, and re-layouts  11.4 us

profile of v2, /device:TPU:5, one launch (start us, length us, event | category | flops | bytes accessed | tf_op | source)
XLA Modules:
  0.0 248.7 jit_solution(6095703666972225959)
XLA Ops:
  0.0 11.4 %copy.10 = bf16[2,128,8,2048]{3,1,0,2:T(8,128)(2,1)} copy(bf16[2,128,8,2048]{3,2,1,0:T(8,128)(2,1)} %param.6) | data formatting | bytes 16777216 | tf_op args[0]
  11.4 225.6 %shard_map.64 = f32[16,8,64,256]{3,2,1,0:T(8,128)} custom-call(bf16[8,2,128,2048]{3,2,1,0:T(8,128)(2,1)} %bitcast.5, bf16[128,128]{1,0:T(8,128)(2,1)} %mix_ref.1, bf16[8,2048]{1,0:T(8,128)(2,1)} %cap_ref.1, s32[8,2048]{1,0:T(8,128)} %live_ref.1, s32[8,32]{1,0:T(8,128)} %where_ref.1, f32[8,32]{1,0:T(8,128)} %speed_ref.1), custom_call_target="tpu_custom_call" | custom-call | tf_op jit(solution)/shard_map/pallas_call | solution.py:453
  237.0 11.6 %copy.8 = f32[64,16,8,256]{3,2,1,0:T(8,128)} copy(f32[64,16,8,256]{3,0,2,1:T(8,128)} %bitcast.4) | data formatting | bytes 16777216 | tf_op jit(solution)/shard_map/transpose | solution.py:495
